TPU v7x, 256 devices: a whole 4x4x8 slice. The times are simulated.
256 devices in a mesh: dp: 8 (over y, core), lang: 32 (over x, z).
Axes of the slice: x: 4, y: 4, z: 8, core: 2. Of those that a mesh axis runs over, the one named last changes fastest.
Arguments:
- inputs: bfloat16 [32768, 2048], P(('dp', 'lang')), may hold values from -6 to 6
- grad_out: bfloat16 [32768, 2048], P(('dp', 'lang')), may hold values from -6 to 6
- lang_ids: int32 [32768], P(('dp', 'lang')), may hold values from 0 to 199, as said below
- lang_block: int32 [200], replicated, may hold values from 0 to 31, as said below
- block_owner: int32 [32], replicated, may hold values from 0 to 31, each once
- w_in: bfloat16 [32, 4096, 2048], P('lang', 'dp'), may hold values from -0.125 to 0.125
- w_out: bfloat16 [32, 4096, 2048], P('lang', 'dp'), may hold values from -0.09375 to 0.09375
Outputs:
- grad_in: bfloat16 [32768, 2048], P(('dp', 'lang'))
- grad_w_in: bfloat16 [32, 4096, 2048], P('lang', 'dp')
- grad_w_out: bfloat16 [32, 4096, 2048], P('lang', 'dp')
Inputs may be any that keep to these rules, and one draw needn't show every extreme that they name: `lang_ids`: through lang_block, the 128 rows of one device name any one block at most 5 times; in every draw one block is named exactly 5 times by the rows of every device. `lang_block`: every block has at least one language. A permutation: block b's weights and gradients sit at index block_owner[b] of the block dimension.
All inputs are finite; a program needn't handle non-finite values.
Results may differ from a plain program's by a relative error of at most 0.019.
Values may be sent and summed in bfloat16 or wider, within the bound.
A program may use at most 128 MiB of HBM per device.

v0:
```python
import math
import jax
import jax.numpy as jnp
from jax import lax
from jax.sharding import PartitionSpec as P

gelu_scale = math.sqrt(2.0 / math.pi)
CAP = 5


def gelu_parts(pre_act):
    tanh_arg = gelu_scale * (pre_act + 0.044715 * pre_act * pre_act * pre_act)
    tangent = jnp.tanh(tanh_arg)
    gelu_value = 0.5 * pre_act * (1.0 + tangent)
    gelu_slope = 0.5 * (1.0 + tangent) + 0.5 * pre_act * (1.0 - tangent * tangent) * gelu_scale * (
        1.0 + 3.0 * 0.044715 * pre_act * pre_act
    )
    return (gelu_value, gelu_slope)


def local_grads(rows_x, rows_g, w_first, w_second):
    pre_act = jnp.dot(rows_x, w_first.T, preferred_element_type=jnp.float32)
    gelu_value, gelu_slope = gelu_parts(pre_act)
    activated = gelu_value.astype(jnp.bfloat16)
    back_grad = jnp.dot(rows_g, w_second.T, preferred_element_type=jnp.float32)
    pre_grad = (back_grad * gelu_slope).astype(jnp.bfloat16)
    g_out = jnp.dot(activated.T, rows_g, preferred_element_type=jnp.float32).astype(jnp.bfloat16)
    g_in = jnp.dot(pre_grad.T, rows_x, preferred_element_type=jnp.float32).astype(jnp.bfloat16)
    return (pre_grad, g_in, g_out)


def slots_of(lang_ids, lang_block, block_owner):
    rows = lang_ids.shape[0]
    holder_of_lang = jnp.sum(
        jnp.where(
            lang_block[:, None] == jnp.arange(block_owner.shape[0])[None, :],
            block_owner[None, :],
            0,
        ),
        axis=1,
    )
    holder = jnp.sum(
        jnp.where(
            lang_ids[:, None] == jnp.arange(lang_block.shape[0])[None, :],
            holder_of_lang[None, :],
            0,
        ),
        axis=1,
    )
    row = jnp.arange(rows)
    earlier = jnp.sum(
        ((holder[:, None] == holder[None, :]) & (row[None, :] < row[:, None])).astype(jnp.int32),
        axis=1,
    )
    return holder * CAP + earlier


def body(inputs, grad_out, lang_ids, lang_block, block_owner, w_in, w_out):
    feat = inputs.shape[1]
    n_lang = lax.axis_size("lang")
    slots = n_lang * CAP
    position = slots_of(lang_ids, lang_block, block_owner)
    onehot = (position[None, :] == jnp.arange(slots)[:, None]).astype(jnp.bfloat16)
    packed = jnp.concatenate([inputs, grad_out], axis=1)
    outgoing = jnp.dot(onehot, packed, preferred_element_type=jnp.float32).astype(jnp.bfloat16)
    outgoing = outgoing.reshape(n_lang, CAP * 2 * feat // 128, 128)
    arrived = lax.all_to_all(outgoing, "lang", split_axis=0, concat_axis=0, tiled=True)
    arrived = arrived.reshape(slots, 2 * feat)
    gathered = lax.all_gather(arrived, "dp", axis=0, tiled=True)
    pre_grad, g_in, g_out = local_grads(gathered[:, :feat], gathered[:, feat:], w_in[0], w_out[0])
    partial_dx = jnp.dot(pre_grad, w_in[0], preferred_element_type=jnp.float32).astype(jnp.bfloat16)
    summed = lax.psum_scatter(partial_dx, "dp", scatter_dimension=0, tiled=True)
    back = summed.reshape(n_lang, CAP * feat // 128, 128)
    returned = lax.all_to_all(back, "lang", split_axis=0, concat_axis=0, tiled=True)
    returned = returned.reshape(slots, feat)
    grad_in = jnp.dot(onehot.T, returned, preferred_element_type=jnp.float32).astype(jnp.bfloat16)
    return (grad_in, g_in[None], g_out[None])


def solution(mesh):
    in_specs = (
        P(("dp", "lang"), None),
        P(("dp", "lang"), None),
        P(("dp", "lang")),
        P(),
        P(),
        P("lang", "dp", None),
        P("lang", "dp", None),
    )
    out_specs = (P(("dp", "lang"), None), P("lang", "dp", None), P("lang", "dp", None))
    return jax.shard_map(body, mesh=mesh, in_specs=in_specs, out_specs=out_specs, check_vma=False)
```

profile of v0, /device:TPU:32, one launch (start us, length us, event | category | flops | bytes accessed | tf_op | source)
XLA Modules:
  0.0 218.1 jit_solution(15846784867144905162)
XLA Ops:
  7.2 0.0 copy-start
  7.2 0.0 all-gather.2.cloned.1.call-start
  7.2 0.9 select_reduce_fusion.1
  8.2 0.8 select_reduce_fusion
  8.9 0.2 convert_reduce_fusion
  9.1 2.8 %convolution_convert_fusion.1 = bf16[160,4096]{1,0:T(8,128)(2,1)} fusion(bf16[128,2048]{1,0:T(8,128)(2,1)} %param.8, bf16[128,2048]{1,0:T(8,128)(2,1)} %param.7, s32[128]{0:T(128)S(1)} %multiply_add_fusion.1), kind=kOutput, calls=%fused_computation.1 | convolution fusion | flops 170545152 | bytes 2359808 | tf_op jit(solution)/shard_map/dot_general | solution.py:65
  11.9 2.4 %reshape.30 = bf16[32,160,128]{2,1,0:T(8,128)(2,1)S(1)} reshape(bf16[160,4096]{1,0:T(8,128)(2,1)} %convolution_convert_fusion.1) | data formatting | bytes 2621440 | tf_op jit(solution)/shard_map/reshape | solution.py:66
  14.3 45.8 %all_to_all.10 = bf16[32,160,128]{2,1,0:T(8,128)(2,1)} all-to-all(bf16[32,160,128]{2,1,0:T(8,128)(2,1)S(1)} %reshape.30), channel_id=1, replica_groups=mesh['dp'=8,'lang'=32] {'lang'}, dimensions={0} | all-to-all | bytes 2621440 | tf_op jit(solution)/shard_map/all_to_all | solution.py:67
  60.1 3.2 %reshape.31 = bf16[160,4096]{1,0:T(8,128)(2,1)} reshape(bf16[32,160,128]{2,1,0:T(8,128)(2,1)} %all_to_all.10) | data formatting | bytes 2621440 | tf_op jit(solution)/shard_map/reshape | solution.py:68
  63.3 0.0 all-gather.2.cloned.1.call-update
  63.3 0.0 reduce-scatter.2.cloned.1.call-start
  63.4 57.2 %all-gather.2.cloned.1.call-done = bf16[1280,4096]{1,0:T(8,128)(2,1)} async-done(((bf16[160,4096]{1,0:T(8,128)(2,1)}), bf16[1280,4096]{1,0:T(8,128)(2,1)}) %all-gather.2.cloned.1.call-update) | async-done | bytes 10485776 | tf_op jit(solution)/shard_map/all_gather | solution.py:69
  120.6 0.0 copy-done
  120.6 0.0 copy-start.1
  120.6 0.0 copy-start.2
  120.6 5.0 %fusion.2 = f32[1280,512]{1,0:T(8,128)S(1)} fusion(bf16[1280,4096]{1,0:T(8,128)(2,1)} %all-gather.2.cloned.1.call-done, bf16[1,512,2048]{2,1,0:T(8,128)(2,1)S(1)} %copy-done), kind=kOutput, calls=%fused_computation.4 | convolution fusion | flops 2684354560 | bytes 9961472 | tf_op jit(solution)/shard_map/dot_general | solution.py:22
  125.7 0.5 copy-done.1
  126.2 0.6 copy-done.2
  126.8 0.0 copy-start.3
  126.8 4.3 %fusion.11 = bf16[1280,512]{1,0:T(8,128)(2,1)S(1)} fusion(bf16[1280,4096]{1,0:T(8,128)(2,1)S(1)} %copy-done.1, f32[1280,512]{1,0:T(8,128)S(1)} %fusion.2, bf16[1,512,2048]{2,1,0:T(8,128)(2,1)S(1)} %copy-done.2), kind=kOutput, calls=%fused_computation.13 | convolution fusion | flops 2696806400 | bytes 11272192 | tf_op jit(solution)/shard_map/dot_general | solution.py:25
  131.1 0.0 copy-done.3
  131.1 0.0 copy-start.5
  131.1 1.0 copy-done.5
  132.1 4.7 %convolution_convert_fusion = bf16[1280,2048]{1,0:T(8,128)(2,1)} fusion(bf16[1280,512]{1,0:T(8,128)(2,1)S(1)} %fusion.11, bf16[1,512,2048]{2,1,0:T(8,128)(2,1)S(1)} %copy-done), kind=kOutput, calls=%fused_computation | convolution fusion | flops 2686976000 | bytes 8650752 | tf_op jit(solution)/shard_map/dot_general | solution.py:71
  136.8 0.0 reduce-scatter.2.cloned.1.call-update
  136.8 43.0 %reduce-scatter.2.cloned.1.call-done = bf16[160,2048]{1,0:T(8,128)(2,1)} async-done(((bf16[1280,2048]{1,0:T(8,128)(2,1)}), bf16[160,2048]{1,0:T(8,128)(2,1)}) %reduce-scatter.2.cloned.1.call-update) | async-done | bytes 655376 | tf_op jit(solution)/shard_map/reduce_scatter | solution.py:72
  179.8 2.1 reshape.32
  181.9 10.1 %all-to-all-start.1 = ((bf16[32,80,128]{2,1,0:T(8,128)(2,1)}), bf16[32,80,128]{2,1,0:T(8,128)(2,1)S(1)}, u32[]{:S(2)}, u32[]{:S(2)}) async-start(bf16[32,80,128]{2,1,0:T(8,128)(2,1)} %reshape.32), calls=%async_computation.2 | async-start | bytes 1310720 | tf_op jit(solution)/shard_map/all_to_all | solution.py:74
  192.0 0.0 copy-start.4
  192.0 7.3 %fusion.20 = bf16[1,512,2048]{2,1,0:T(8,128)(2,1)} fusion(bf16[1280,512]{1,0:T(8,128)(2,1)} %copy-done.5, bf16[1280,4096]{1,0:T(8,128)(2,1)} %all-gather.2.cloned.1.call-done), kind=kOutput, calls=%fused_computation.16 | convolution fusion | flops 2685403136 | bytes 8650752 | tf_op jit(solution)/shard_map/dot_general | solution.py:28
  199.3 0.0 copy-done.4
  199.3 6.7 %fusion.23 = bf16[1,512,2048]{2,1,0:T(8,128)(2,1)} fusion(bf16[1280,4096]{1,0:T(8,128)(2,1)} %all-gather.2.cloned.1.call-done, f32[1280,512]{1,0:T(8,128)S(1)} %copy-done.4), kind=kOutput, calls=%fused_computation.17 | convolution fusion | flops 2691301376 | bytes 9961472 | tf_op jit(solution)/shard_map/dot_general | solution.py:27
  206.0 3.8 %all-to-all-done.1 = bf16[32,80,128]{2,1,0:T(8,128)(2,1)S(1)} async-done(((bf16[32,80,128]{2,1,0:T(8,128)(2,1)}), bf16[32,80,128]{2,1,0:T(8,128)(2,1)S(1)}, u32[]{:S(2)}, u32[]{:S(2)}) %all-to-all-start.1) | async-done | bytes 655392 | tf_op jit(solution)/shard_map/all_to_all | solution.py:74
  209.8 0.3 reshape.33
  210.1 1.1 convolution_convert_fusion.2
  (1 shorter events, 0.0 us)
Async XLA Ops:
  7.2 113.5 %copy-start = (bf16[1,512,2048]{2,1,0:T(8,128)(2,1)S(1)}, bf16[1,512,2048]{2,1,0:T(8,128)(2,1)}, u32[]{:S(2)}) copy-start(bf16[1,512,2048]{2,1,0:T(8,128)(2,1)} %param.12) | copy-start | bytes 6291460
  7.2 113.4 %all-gather.2.cloned.1.call-start = ((), (), s32[]{:S(2)}) async-start(), calls=%async_computation.3 | async-start | bytes 11796480 | tf_op jit(solution)/shard_map/all_gather | solution.py:69
  63.3 116.5 %reduce-scatter.2.cloned.1.call-start = ((), (), s32[]{:S(2)}) async-start(), calls=%async_computation.4 | async-start | bytes 5898240 | tf_op jit(solution)/shard_map/reduce_scatter | solution.py:72
  120.6 5.5 %copy-start.1 = (bf16[1280,4096]{1,0:T(8,128)(2,1)S(1)}, bf16[1280,4096]{1,0:T(8,128)(2,1)}, u32[]{:S(2)}) copy-start(bf16[1280,4096]{1,0:T(8,128)(2,1)} %all-gather.2.cloned.1.call-done) | copy-start | bytes 31457284
  120.6 6.1 %copy-start.2 = (bf16[1,512,2048]{2,1,0:T(8,128)(2,1)S(1)}, bf16[1,512,2048]{2,1,0:T(8,128)(2,1)}, u32[]{:S(2)}) copy-start(bf16[1,512,2048]{2,1,0:T(8,128)(2,1)} %param.13) | copy-start | bytes 6291460
  126.8 4.3 %copy-start.3 = (f32[1280,512]{1,0:T(8,128)}, f32[1280,512]{1,0:T(8,128)S(1)}, u32[]{:S(2)}) copy-start(f32[1280,512]{1,0:T(8,128)S(1)} %fusion.2) | copy-start | bytes 7864324
  131.1 1.1 copy-start.5
  181.9 27.9 %all-to-all-start.1 = ((bf16[32,80,128]{2,1,0:T(8,128)(2,1)}), bf16[32,80,128]{2,1,0:T(8,128)(2,1)S(1)}, u32[]{:S(2)}, u32[]{:S(2)}) async-start(bf16[32,80,128]{2,1,0:T(8,128)(2,1)} %reshape.32), calls=%async_computation.2 | async-start | bytes 1310720 | tf_op jit(solution)/shard_map/all_to_all | solution.py:74
  192.0 7.3 %copy-start.4 = (f32[1280,512]{1,0:T(8,128)S(1)}, f32[1280,512]{1,0:T(8,128)}, u32[]{:S(2)}) copy-start(f32[1280,512]{1,0:T(8,128)} %copy-done.3) | copy-start | bytes 7864324
Sparse Core Ops, SparseCore 0:
  63.4 57.1 all-gather.1
  136.9 42.8 reduce-scatter.1
where the time goes:
time: 219 us; the launch traced here: 218 us
  waiting for transfers between devices  104 us (47%)
  blocking collectives  45.8 us (21%)
  matrix products  31.9 us (15%)
  between operations  14.1 us (6%)
  local copies, waits for them, and re-layouts  10.2 us (5%)
  starting transfers between devices  10.1 us (5%)
    all_gather x1, waiting for transfers between devices, body(): gathered = lax.all_gather(arrived, 'dp', axis=0, tiled=True)  57.2 us
    all_to_all x1, blocking collectives, body(): lax.all_to_all(outgoing, 'lang', split_axis=0, concat_axis=0, tiled=True)  45.8 us
    reduce_scatter x1, waiting for transfers between devices, body(): summed = lax.psum_scatter(partial_dx, 'dp', scatter_dimension=0, tiled=True)  43 us
    all_to_all x1, starting transfers between devices, body(): lax.all_to_all(back, 'lang', split_axis=0, concat_axis=0, tiled=True)  10.1 us
    dot_general x1, matrix products, local_grads(): jnp.dot(pre_grad.T, rows_x, preferred_element_type=jnp.float32)  7.27 us
    dot_general x1, matrix products, local_grads(): jnp.dot(activated.T, rows_g, preferred_element_type=jnp.float32)  6.74 us
    dot_general x1, matrix products, local_grads(): pre_act = jnp.dot(rows_x, w_first.T, preferred_element_type=jnp.float32)  5.03 us
    dot_general x1, matrix products, body(): jnp.dot(pre_grad, w_in[0], preferred_element_type=jnp.float32)  4.66 us
  transfers between devices with their start and end apart: 3, of which 3 were waited for; matrix products, arithmetic and copies ran while one was open for 6% of the time, Pallas kernels for 0%

commit v1 on v0

--- a/solution.py
+++ b/solution.py
@@ -66,7 +66,9 @@
     outgoing = outgoing.reshape(n_lang, CAP * 2 * feat // 128, 128)
     arrived = lax.all_to_all(outgoing, "lang", split_axis=0, concat_axis=0, tiled=True)
     arrived = arrived.reshape(slots, 2 * feat)
-    gathered = lax.all_gather(arrived, "dp", axis=0, tiled=True)
+    gathered = jnp.concatenate(
+        lax.all_to_all(jnp.stack([arrived] * lax.axis_size("dp")), "dp", 0, 0), axis=0
+    )
     pre_grad, g_in, g_out = local_grads(gathered[:, :feat], gathered[:, feat:], w_in[0], w_out[0])
     partial_dx = jnp.dot(pre_grad, w_in[0], preferred_element_type=jnp.float32).astype(jnp.bfloat16)
     summed = lax.psum_scatter(partial_dx, "dp", scatter_dimension=0, tiled=True)

time: 219 us -> 281 us (1.28)
  blocking collectives: 45.8 us -> 169 us
  waiting for transfers between devices: 104 us -> 40.4 us
  local copies, waits for them, and re-layouts: 10.2 us -> 14.8 us
    all_to_all x0 -> x1, blocking collectives: none -> 123 us  [body(): lax.all_to_all(jnp.stack([arrived] * lax.axis_size('dp')), 'dp', 0, 0)]
    all_gather x1 -> x0, waiting for transfers between devices: 57.2 us -> none  [body(): gathered = lax.all_gather(arrived, 'dp', axis=0, tiled=True)]
    another operation x0 -> x2, local copies, waits for them, and re-layouts: none -> 7.68 us  [body(): jnp.stack([arrived] * lax.axis_size('dp'))]
    reduce_scatter x1, waiting for transfers between devices: 43 us -> 36.6 us  [body(): summed = lax.psum_scatter(partial_dx, 'dp', scatter_dimension=0, tiled=True)]
    reshape x1 -> x0, local copies, waits for them, and re-layouts: 3.24 us -> none  [body(): arrived = arrived.reshape(slots, 2 * feat)]
  transfers between devices with their start and end apart: 3 -> 2, of which waited for: 3 -> 2; matrix products, arithmetic and copies ran while one was open for 6% -> 5% of each run, Pallas kernels for 0% -> 0%
where the time goes in v1:
time: 281 us; the launch traced here: 280 us
  blocking collectives  169 us (60%)
  waiting for transfers between devices  40.4 us (14%)
  matrix products  29.8 us (11%)
  local copies, waits for them, and re-layouts  14.8 us (5%)
  between operations  14.1 us (5%)
  starting transfers between devices  10.1 us (4%)
    all_to_all x1, blocking collectives, body(): lax.all_to_all(jnp.stack([arrived] * lax.axis_size('dp')), 'dp', 0, 0)  123 us
    all_to_all x1, blocking collectives, body(): lax.all_to_all(outgoing, 'lang', split_axis=0, concat_axis=0, tiled=True)  45.8 us
    reduce_scatter x1, waiting for transfers between devices, body(): summed = lax.psum_scatter(partial_dx, 'dp', scatter_dimension=0, tiled=True)  36.6 us
    all_to_all x1, starting transfers between devices, body(): lax.all_to_all(back, 'lang', split_axis=0, concat_axis=0, tiled=True)  10.1 us
    another operation x2, local copies, waits for them, and re-layouts, body(): jnp.stack([arrived] * lax.axis_size('dp'))  7.68 us
    dot_general x1, matrix products, local_grads(): jnp.dot(pre_grad.T, rows_x, preferred_element_type=jnp.float32)  7.27 us
    dot_general x1, matrix products, local_grads(): jnp.dot(activated.T, rows_g, preferred_element_type=jnp.float32)  6.81 us
  transfers between devices with their start and end apart: 2, of which 2 were waited for; matrix products, arithmetic and copies ran while one was open for 5% of the time, Pallas kernels for 0%

profile of v1, /device:TPU:32, one launch (start us, length us, event | category | flops | bytes accessed | tf_op | source)
XLA Modules:
  0.0 280.2 jit_solution(5785718043892843427)
XLA Ops:
  7.2 0.0 copy-start
  7.2 0.0 reduce-scatter.2.cloned.1.call-start
  7.2 0.9 select_reduce_fusion.1
  8.2 0.8 select_reduce_fusion
  8.9 0.2 convert_reduce_fusion
  9.1 2.8 convolution_convert_fusion.1
  11.9 2.4 reshape.32
  14.3 45.8 %all_to_all.15 = bf16[32,160,128]{2,1,0:T(8,128)(2,1)} all-to-all(bf16[32,160,128]{2,1,0:T(8,128)(2,1)S(1)} %reshape.32), channel_id=1, replica_groups=mesh['dp'=8,'lang'=32] {'lang'}, dimensions={0} | all-to-all | bytes 2621440 | tf_op jit(solution)/shard_map/all_to_all | solution.py:67
  60.1 2.4 stack_reshape.2
  62.4 5.3 %stack.3 = bf16[8,160,4096]{2,1,0:T(8,128)(2,1)} broadcast(bf16[160,4096]{1,0:T(8,128)(2,1)S(1)} %stack_reshape.2), dimensions={1,2} | broadcast | bytes 11796480 | tf_op jit(solution)/shard_map/stack | solution.py:70
  67.7 123.2 %all_to_all.16 = bf16[8,160,4096]{2,1,0:T(8,128)(2,1)S(1)} all-to-all(bf16[8,160,4096]{2,1,0:T(8,128)(2,1)} %stack.3), channel_id=1, replica_groups=mesh['dp'=8,'lang'=32] {'dp'}, dimensions={0} | all-to-all | bytes 20971520 | tf_op jit(solution)/shard_map/all_to_all | solution.py:70
  191.0 0.0 copy-start.1
  191.0 0.0 copy-done
  191.0 0.0 copy-start.2
  191.0 2.9 %fusion.2 = f32[1280,512]{1,0:T(8,128)S(1)} fusion(bf16[1280,4096]{1,0:T(8,128)(2,1)S(1)} %bitcast.16, bf16[1,512,2048]{2,1,0:T(8,128)(2,1)S(1)} %copy-done), kind=kOutput, calls=%fused_computation.4 | convolution fusion | flops 2684354560 | bytes 9961472 | tf_op jit(solution)/shard_map/dot_general | solution.py:22
  193.9 1.3 copy-done.1
  195.2 0.0 copy-done.2
  195.2 0.0 copy-start.3
  195.2 4.3 %fusion.11 = bf16[1280,512]{1,0:T(8,128)(2,1)S(1)} fusion(bf16[1280,4096]{1,0:T(8,128)(2,1)S(1)} %bitcast.17, f32[1280,512]{1,0:T(8,128)S(1)} %fusion.2, bf16[1,512,2048]{2,1,0:T(8,128)(2,1)S(1)} %copy-done.2), kind=kOutput, calls=%fused_computation.13 | convolution fusion | flops 2696806400 | bytes 11272192 | tf_op jit(solution)/shard_map/dot_general | solution.py:25
  199.5 0.0 copy-done.3
  199.5 0.0 copy-start.5
  199.5 1.0 copy-done.5
  200.6 4.6 %convolution_convert_fusion = bf16[1280,2048]{1,0:T(8,128)(2,1)} fusion(bf16[1280,512]{1,0:T(8,128)(2,1)S(1)} %fusion.11, bf16[1,512,2048]{2,1,0:T(8,128)(2,1)S(1)} %copy-done), kind=kOutput, calls=%fused_computation | convolution fusion | flops 2686976000 | bytes 8650752 | tf_op jit(solution)/shard_map/dot_general | solution.py:73
  205.2 0.0 reduce-scatter.2.cloned.1.call-update
  205.2 36.6 %reduce-scatter.2.cloned.1.call-done = bf16[160,2048]{1,0:T(8,128)(2,1)} async-done(((bf16[1280,2048]{1,0:T(8,128)(2,1)}), bf16[160,2048]{1,0:T(8,128)(2,1)}) %reduce-scatter.2.cloned.1.call-update) | async-done | bytes 655376 | tf_op jit(solution)/shard_map/reduce_scatter | solution.py:74
  241.8 2.2 reshape.34
  243.9 10.1 %all-to-all-start.2 = ((bf16[32,80,128]{2,1,0:T(8,128)(2,1)}), bf16[32,80,128]{2,1,0:T(8,128)(2,1)S(1)}, u32[]{:S(2)}, u32[]{:S(2)}) async-start(bf16[32,80,128]{2,1,0:T(8,128)(2,1)} %reshape.34), calls=%async_computation.3 | async-start | bytes 1310720 | tf_op jit(solution)/shard_map/all_to_all | solution.py:76
  254.0 0.0 copy-start.4
  254.0 7.3 %fusion.20 = bf16[1,512,2048]{2,1,0:T(8,128)(2,1)} fusion(bf16[1280,512]{1,0:T(8,128)(2,1)} %copy-done.5, bf16[1280,4096]{1,0:T(8,128)(2,1)} %bitcast.18), kind=kOutput, calls=%fused_computation.16 | convolution fusion | flops 2685403136 | bytes 8650752 | tf_op jit(solution)/shard_map/dot_general | solution.py:28
  261.3 0.0 copy-done.4
  261.3 6.8 %fusion.23 = bf16[1,512,2048]{2,1,0:T(8,128)(2,1)} fusion(bf16[1280,4096]{1,0:T(8,128)(2,1)} %bitcast.19, f32[1280,512]{1,0:T(8,128)S(1)} %copy-done.4), kind=kOutput, calls=%fused_computation.17 | convolution fusion | flops 2691301376 | bytes 9961472 | tf_op jit(solution)/shard_map/dot_general | solution.py:27
  268.1 3.8 %all-to-all-done.2 = bf16[32,80,128]{2,1,0:T(8,128)(2,1)S(1)} async-done(((bf16[32,80,128]{2,1,0:T(8,128)(2,1)}), bf16[32,80,128]{2,1,0:T(8,128)(2,1)S(1)}, u32[]{:S(2)}, u32[]{:S(2)}) %all-to-all-start.2) | async-done | bytes 655392 | tf_op jit(solution)/shard_map/all_to_all | solution.py:76
  271.9 0.3 reshape.35
  272.2 1.1 convolution_convert_fusion.2
  (1 shorter events, 0.0 us)
Async XLA Ops:
  7.2 183.8 %copy-start = (bf16[1,512,2048]{2,1,0:T(8,128)(2,1)S(1)}, bf16[1,512,2048]{2,1,0:T(8,128)(2,1)}, u32[]{:S(2)}) copy-start(bf16[1,512,2048]{2,1,0:T(8,128)(2,1)} %param.12) | copy-start | bytes 6291460
  7.2 234.6 %reduce-scatter.2.cloned.1.call-start = ((), (), s32[]{:S(2)}) async-start(), calls=%async_computation.4 | async-start | bytes 5898240 | tf_op jit(solution)/shard_map/reduce_scatter | solution.py:74
  191.0 4.2 %copy-start.1 = (bf16[8,160,4096]{2,1,0:T(8,128)(2,1)}, bf16[8,160,4096]{2,1,0:T(8,128)(2,1)S(1)}, u32[]{:S(2)}) copy-start(bf16[8,160,4096]{2,1,0:T(8,128)(2,1)S(1)} %all_to_all.16) | copy-start | bytes 31457284
  191.0 4.2 %copy-start.2 = (bf16[1,512,2048]{2,1,0:T(8,128)(2,1)S(1)}, bf16[1,512,2048]{2,1,0:T(8,128)(2,1)}, u32[]{:S(2)}) copy-start(bf16[1,512,2048]{2,1,0:T(8,128)(2,1)} %param.13) | copy-start | bytes 6291460
  195.2 4.3 %copy-start.3 = (f32[1280,512]{1,0:T(8,128)}, f32[1280,512]{1,0:T(8,128)S(1)}, u32[]{:S(2)}) copy-start(f32[1280,512]{1,0:T(8,128)S(1)} %fusion.2) | copy-start | bytes 7864324
  199.5 1.1 copy-start.5
  243.9 27.9 %all-to-all-start.2 = ((bf16[32,80,128]{2,1,0:T(8,128)(2,1)}), bf16[32,80,128]{2,1,0:T(8,128)(2,1)S(1)}, u32[]{:S(2)}, u32[]{:S(2)}) async-start(bf16[32,80,128]{2,1,0:T(8,128)(2,1)} %reshape.34), calls=%async_computation.3 | async-start | bytes 1310720 | tf_op jit(solution)/shard_map/all_to_all | solution.py:76
  254.0 7.3 %copy-start.4 = (f32[1280,512]{1,0:T(8,128)S(1)}, f32[1280,512]{1,0:T(8,128)}, u32[]{:S(2)}) copy-start(f32[1280,512]{1,0:T(8,128)} %copy-done.3) | copy-start | bytes 7864324
Sparse Core Ops, SparseCore 0:
  205.3 36.4 reduce-scatter.1
